TPU v7x, 256 devices: a whole 4x4x8 slice. The times are simulated.
256 devices in a mesh: row: 16 (over y, x), col: 16 (over z, core).
Axes of the slice: x: 4, y: 4, z: 8, core: 2. Of those that a mesh axis runs over, the one named last changes fastest.
Arguments:
- slab: float32 [32768, 16384], P('row', 'col'), may hold values from -30 to 30, as said below
- test_matrix: float32 [16384, 128], P('col'), may hold values from -0.046875 to 0.046875
Outputs:
- basis: float32 [32768, 128], P(('row', 'col'))
- r_factor: float32 [128, 128], replicated
Inputs may be any that keep to these rules, and one draw needn't show every extreme that they name: `slab`: the sketch's condition number (largest over smallest singular value) is at most 2000.
All inputs are finite; a program needn't handle non-finite values.
Results may differ from a plain program's by a relative error of at most 0.0003.
Values sent between devices are 32-bit elements; how exact they have to be, the bound alone decides.
No kernel may reach another device: no remote copies, remote signals or barrier semaphores. Data moves between devices by JAX's collectives and lax.ppermute only.
A program may use at most 64 MiB of HBM per device.

v0:
```python
import math
import jax
import jax.numpy as jnp
from jax import lax
from jax.sharding import PartitionSpec as P

HIGHEST = lax.Precision.HIGHEST
CONTRACT = (((0,), (0,)), ((), ()))


def gram_of(matrix):
    return lax.dot_general(
        matrix, matrix, CONTRACT, precision=HIGHEST, preferred_element_type=jnp.float32
    )


def orthonormal(matrix, summed):
    lower_one = jnp.linalg.cholesky(summed(gram_of(matrix)))
    inner = lax.linalg.triangular_solve(
        lower_one, matrix, left_side=False, lower=True, transpose_a=True
    )
    lower_two = jnp.linalg.cholesky(summed(gram_of(inner)))
    result = lax.linalg.triangular_solve(
        lower_two, inner, left_side=False, lower=True, transpose_a=True
    )
    factor = jnp.dot(
        lower_two.T, lower_one.T, precision=HIGHEST, preferred_element_type=jnp.float32
    )
    return (result, factor)


def sum_everywhere(gram):
    return lax.psum(gram, ("row", "col"))


def local(slab, test_matrix):
    row_total = slab.shape[0] * lax.axis_size("row")
    root_rows = math.sqrt(row_total)
    partial_value = jnp.dot(
        slab, test_matrix, precision=HIGHEST, preferred_element_type=jnp.float32
    )
    sketch_one = lax.psum(partial_value, "col")
    pulled_part = lax.dot_general(
        slab, sketch_one, CONTRACT, precision=HIGHEST, preferred_element_type=jnp.float32
    )
    pulled = lax.psum(pulled_part, "row") / row_total
    owned = lax.psum_scatter(
        jnp.dot(slab, pulled, precision=HIGHEST, preferred_element_type=jnp.float32),
        "col",
        scatter_dimension=0,
        tiled=True,
    )
    result, factor = orthonormal(owned, sum_everywhere)
    return (result * root_rows, factor / root_rows)


def solution(mesh):
    in_specs = (P("row", "col"), P("col", None))
    out_specs = (P(("row", "col"), None), P())
    return jax.shard_map(local, mesh=mesh, in_specs=in_specs, out_specs=out_specs, check_vma=False)
```

profile of v0, /device:TPU:1, one launch (start us, length us, event | category | flops | bytes accessed | tf_op | source)
XLA Modules:
  0.0 847.2 jit_solution(4430770114689326085)
XLA Ops:
  7.2 0.0 copy-start
  7.2 0.0 all-reduce.5.cloned.1.call-start
  7.2 1.0 copy-done
  8.2 9.8 %fusion.22 = f32[2048,128]{1,0:T(8,128)} fusion(f32[2048,1024]{1,0:T(8,128)} %param.5, f32[1024,128]{1,0:T(8,128)S(1)} %copy-done), kind=kOutput, calls=%fused_computation.33 | convolution fusion | flops 3221225472 | bytes 9961472 | tf_op jit(solution)/shard_map/dot_general | solution.py:39
  18.1 0.0 all-reduce.5.cloned.1.call-update
  18.1 0.0 all-reduce.7.cloned.1.call-start
  18.1 115.1 %all-reduce.5.cloned.1.call-done = f32[2048,128]{1,0:T(8,128)} async-done(((f32[2048,128]{1,0:T(8,128)}), f32[2048,128]{1,0:T(8,128)}) %all-reduce.5.cloned.1.call-update) | async-done | bytes 1048592 | tf_op jit(solution)/shard_map/psum | solution.py:42
  133.2 9.2 %convolution_bitcast_fusion.1 = f32[1024,128]{0,1:T(8,128)} fusion(f32[2048,128]{1,0:T(8,128)} %all-reduce.5.cloned.1.call-done, f32[2048,1024]{1,0:T(8,128)} %param.5), kind=kOutput, calls=%fused_computation.1 | convolution fusion | flops 3221225472 | bytes 9961472 | tf_op jit(solution)/shard_map/dot_general | solution.py:43
  142.4 0.0 all-reduce.7.cloned.1.call-update
  142.4 0.2 reduce-scatter.2.cloned.1.call-start
  142.7 94.3 %all-reduce.7.cloned.1.call-done = f32[1024,128]{0,1:T(8,128)} async-done(((f32[1024,128]{0,1:T(8,128)}), f32[1024,128]{0,1:T(8,128)}) %all-reduce.7.cloned.1.call-update) | async-done | bytes 524304 | tf_op jit(solution)/shard_map/psum | solution.py:46
  236.9 13.0 %convolution_bitcast_fusion = f32[2048,128]{0,1:T(8,128)} fusion(f32[2048,1024]{1,0:T(8,128)} %param.5, f32[1024,128]{0,1:T(8,128)} %all-reduce.7.cloned.1.call-done), kind=kOutput, calls=%fused_computation | convolution fusion | flops 3221356544 | bytes 9961472 | tf_op jit(solution)/shard_map/dot_general | solution.py:48
  249.9 0.0 reduce-scatter.2.cloned.1.call-update
  249.9 0.0 all-reduce.9.cloned.1.call-start
  250.0 55.4 %reduce-scatter.2.cloned.1.call-done = f32[128,128]{0,1:T(8,128)} async-done(((f32[2048,128]{0,1:T(8,128)}), f32[128,128]{0,1:T(8,128)}) %reduce-scatter.2.cloned.1.call-update) | async-done | bytes 65552 | tf_op jit(solution)/shard_map/reduce_scatter | solution.py:47
  305.3 1.8 fusion.23
  307.1 0.0 all-reduce.9.cloned.1.call-update
  307.2 0.3 all-reduce.11.cloned.1.call-start
  307.4 244.3 %all-reduce.9.cloned.1.call-done = f32[128,128]{0,1:T(8,128)} async-done(((f32[128,128]{0,1:T(8,128)}), f32[128,128]{0,1:T(8,128)}) %all-reduce.9.cloned.1.call-update) | async-done | bytes 65552 | tf_op jit(solution)/shard_map/psum | solution.py:33
  551.7 0.9 copy.5
  552.7 0.9 fusion.6
  553.5 11.7 %cholesky.44 = f32[128,128]{1,0:T(8,128)S(1)} custom-call(f32[128,128]{1,0:T(8,128)S(1)} %fusion.6), custom_call_target="Cholesky" | custom-call | tf_op jit(solution)/shard_map/jit(cholesky)/cholesky | solution.py:18
  565.3 0.6 compare_reduce_fusion.1
  565.9 0.7 fusion.10
  566.6 9.8 %custom-call.6 = f32[1,128,128]{1,2,0:T(8,128)S(1)} custom-call(f32[1,128,128]{2,1,0:T(8,128)S(1)} %fusion.10), custom_call_target="InvertDiagBlocksLowerTriangular" | custom-call | tf_op jit(solution)/shard_map/triangular_solve/custom-call.0 | solution.py:19
  576.4 1.1 convolution_bitcast_fusion.3
  577.5 0.9 fusion.24
  578.4 0.0 all-reduce.11.cloned.1.call-update
  578.4 234.2 %all-reduce.11.cloned.1.call-done = f32[128,128]{0,1:T(8,128)} async-done(((f32[128,128]{0,1:T(8,128)}), f32[128,128]{0,1:T(8,128)}) %all-reduce.11.cloned.1.call-update) | async-done | bytes 65552 | tf_op jit(solution)/shard_map/psum | solution.py:33
  812.6 0.9 copy.7
  813.5 0.9 fusion.4
  814.4 11.7 %cholesky.55 = f32[128,128]{1,0:T(8,128)S(1)} custom-call(f32[128,128]{1,0:T(8,128)S(1)} %fusion.4), custom_call_target="Cholesky" | custom-call | tf_op jit(solution)/shard_map/jit(cholesky)/cholesky | solution.py:22
  826.1 0.7 compare_reduce_fusion
  826.9 2.3 convolution_multiply_fusion
  829.1 0.7 select_bitcast_fusion
  829.8 9.8 %custom-call.7 = f32[1,128,128]{1,2,0:T(8,128)S(1)} custom-call(f32[1,128,128]{2,1,0:T(8,128)S(1)} %select_bitcast_fusion), custom_call_target="InvertDiagBlocksLowerTriangular" | custom-call | tf_op jit(solution)/shard_map/triangular_solve/custom-call.0 | solution.py:23
  839.6 0.3 fusion
  839.9 0.7 copy.8
  (2 shorter events, 0.1 us)
Async XLA Ops:
  7.2 1.0 copy-start
  7.2 126.1 %all-reduce.5.cloned.1.call-start = ((), (), s32[]{:S(2)}) async-start(), calls=%async_computation.1 | async-start | bytes 2097152 | tf_op jit(solution)/shard_map/psum | solution.py:42
  18.1 218.8 %all-reduce.7.cloned.1.call-start = ((), (), s32[]{:S(2)}) async-start(), calls=%async_computation.2 | async-start | bytes 1048576 | tf_op jit(solution)/shard_map/psum | solution.py:46
  142.4 162.9 %reduce-scatter.2.cloned.1.call-start = ((), (), s32[]{:S(2)}) async-start(), calls=%async_computation.3 | async-start | bytes 1114112 | tf_op jit(solution)/shard_map/reduce_scatter | solution.py:47
  249.9 301.8 %all-reduce.9.cloned.1.call-start = ((), (), s32[]{:S(2)}) async-start(), calls=%async_computation.4 | async-start | bytes 131072 | tf_op jit(solution)/shard_map/psum | solution.py:33
  307.2 505.4 %all-reduce.11.cloned.1.call-start = ((), (), s32[]{:S(2)}) async-start(), calls=%async_computation.5 | async-start | bytes 131072 | tf_op jit(solution)/shard_map/psum | solution.py:33
Sparse Core Ops, SparseCore 0:
  18.2 114.9 all-reduce.4
  142.5 94.3 all-reduce.6
  250.1 55.2 reduce-scatter.1
  312.2 239.4 all-reduce.8
  578.6 234.0 all-reduce.10
where the time goes:
time: 848 us; the launch traced here: 847 us
  waiting for transfers between devices  743 us (88%)
  other arithmetic  47.5 us (6%)
  matrix products  38.4 us (5%)
  between operations  13.9 us (2%)
    psum x2, waiting for transfers between devices, sum_everywhere(): return lax.psum(gram, ('row', 'col'))  478 us
    psum x1, waiting for transfers between devices, local(): sketch_one = lax.psum(partial_value, 'col')  115 us
    psum x1, waiting for transfers between devices, local(): pulled = lax.psum(pulled_part, 'row') / row_total  94.3 us
    reduce_scatter x1, waiting for transfers between devices, local(): lax.psum_scatter(jnp.dot(slab, pulled, precision=HIGHEST, preferred_eleme...  55.4 us
  transfers between devices with their start and end apart: 5, of which 5 were waited for; matrix products, arithmetic and copies ran while one was open for 0% of the time, Pallas kernels for 0%

commit v1 on v0

--- a/solution.py
+++ b/solution.py
@@ -1,3 +1,4 @@
+import functools
 import math
 import jax
 import jax.numpy as jnp
@@ -6,6 +7,23 @@
 
 HIGHEST = lax.Precision.HIGHEST
 CONTRACT = (((0,), (0,)), ((), ()))
+
+
+def take_teams_now(m, a_name):
+    world = jax.lax.axis_size(a_name)
+    v_next, carry_in = (m, 0)
+    while 1 << carry_in < world:
+        tall = jax.lax.ppermute(
+            v_next,
+            axis_name=a_name,
+            perm=[(dev_j, dev_j ^ 1 << carry_in) for dev_j in range(world)],
+        )
+        v_next = v_next + tall
+        carry_in = carry_in + 1
+    return v_next
+
+
+drive_threads_over_axis = functools.partial(take_teams_now, a_name="col")
 
 
 def gram_of(matrix):
@@ -39,7 +57,7 @@
     partial_value = jnp.dot(
         slab, test_matrix, precision=HIGHEST, preferred_element_type=jnp.float32
     )
-    sketch_one = lax.psum(partial_value, "col")
+    sketch_one = drive_threads_over_axis(partial_value)
     pulled_part = lax.dot_general(
         slab, sketch_one, CONTRACT, precision=HIGHEST, preferred_element_type=jnp.float32
     )

time: 848 us -> 857 us (1.011)
  starting transfers between devices: 0.61 us -> 10.5 us
    ppermute x0 -> x4, waiting for transfers between devices: none -> 119 us  [take_teams_now(): jax.lax.ppermute(v_next, axis_name=a_name, perm=[(dev_j, dev_j ^ 1 << car...]
    psum x1 -> x0, waiting for transfers between devices: 115 us -> none  [local(): sketch_one = lax.psum(partial_value, 'col')]
    ppermute x0 -> x4, starting transfers between devices: none -> 10.2 us  [take_teams_now(): jax.lax.ppermute(v_next, axis_name=a_name, perm=[(dev_j, dev_j ^ 1 << car...]
  transfers between devices with their start and end apart: 5 -> 8, of which waited for: 5 -> 8; matrix products, arithmetic and copies ran while one was open for 0% -> 0% of each run, Pallas kernels for 0% -> 0%
where the time goes in v1:
time: 857 us; the launch traced here: 856 us
  waiting for transfers between devices  746 us (87%)
  other arithmetic  47.9 us (6%)
  matrix products  34.7 us (4%)
  between operations  13.9 us (2%)
  starting transfers between devices  10.5 us (1%)
    psum x2, waiting for transfers between devices, sum_everywhere(): return lax.psum(gram, ('row', 'col'))  478 us
    ppermute x4, waiting for transfers between devices, take_teams_now(): jax.lax.ppermute(v_next, axis_name=a_name, perm=[(dev_j, dev_j ^ 1 << car...  119 us
    psum x1, waiting for transfers between devices, local(): pulled = lax.psum(pulled_part, 'row') / row_total  93.7 us
    reduce_scatter x1, waiting for transfers between devices, local(): lax.psum_scatter(jnp.dot(slab, pulled, precision=HIGHEST, preferred_eleme...  55.3 us
  transfers between devices with their start and end apart: 8, of which 8 were waited for; matrix products, arithmetic and copies ran while one was open for 0% of the time, Pallas kernels for 0%

profile of v1, /device:TPU:1, one launch (start us, length us, event | category | flops | bytes accessed | tf_op | source)
XLA Modules:
  0.0 856.2 jit_solution(10042275525078849779)
XLA Ops:
  7.2 0.0 copy-start
  7.2 0.0 all-reduce.4.cloned.1.call-start
  7.2 1.0 copy-done
  8.2 0.0 copy-start.1
  8.2 9.9 %fusion.23 = f32[2048,128]{1,0:T(8,128)S(1)} fusion(f32[2048,1024]{1,0:T(8,128)} %param.5, f32[1024,128]{1,0:T(8,128)S(1)} %copy-done), kind=kOutput, calls=%fused_computation.34 | convolution fusion | flops 3221225472 | bytes 9961472 | tf_op jit(solution)/shard_map/dot_general | solution.py:57
  18.1 3.3 collective-permute-start
  21.5 2.3 collective-permute-done
  23.8 0.1 add.28
  23.9 0.1 collective-permute-start.1
  24.0 24.4 %collective-permute-done.1 = f32[2048,128]{1,0:T(8,128)S(1)} collective-permute-done((f32[2048,128]{1,0:T(8,128)S(1)}, f32[2048,128]{1,0:T(8,128)S(1)}, u32[]{:S(2)}, u32[]{:S(2)}) %collective-permute-start.1) | collective-permute-done | bytes 1048608 | tf_op jit(solution)/shard_map/ppermute | solution.py:16
  48.3 0.1 add.29
  48.4 1.7 collective-permute-start.2
  50.1 46.5 %collective-permute-done.2 = f32[2048,128]{1,0:T(8,128)S(1)} collective-permute-done((f32[2048,128]{1,0:T(8,128)S(1)}, f32[2048,128]{1,0:T(8,128)S(1)}, u32[]{:S(2)}, u32[]{:S(2)}) %collective-permute-start.2) | collective-permute-done | bytes 1048608 | tf_op jit(solution)/shard_map/ppermute | solution.py:16
  96.7 0.1 add.30
  96.8 5.1 collective-permute-start.3
  101.8 45.5 %collective-permute-done.3 = f32[2048,128]{1,0:T(8,128)S(1)} collective-permute-done((f32[2048,128]{1,0:T(8,128)S(1)}, f32[2048,128]{1,0:T(8,128)S(1)}, u32[]{:S(2)}, u32[]{:S(2)}) %collective-permute-start.3) | collective-permute-done | bytes 1048608 | tf_op jit(solution)/shard_map/ppermute | solution.py:16
  147.3 0.0 copy-done.1
  147.3 5.5 convolution_bitcast_fusion.1
  152.7 0.0 all-reduce.4.cloned.1.call-update
  152.8 0.2 reduce-scatter.2.cloned.1.call-start
  153.0 93.7 %all-reduce.4.cloned.1.call-done = f32[1024,128]{0,1:T(8,128)} async-done(((f32[1024,128]{0,1:T(8,128)}), f32[1024,128]{0,1:T(8,128)}) %all-reduce.4.cloned.1.call-update) | async-done | bytes 524304 | tf_op jit(solution)/shard_map/psum | solution.py:64
  246.7 13.0 %convolution_bitcast_fusion = f32[2048,128]{0,1:T(8,128)} fusion(f32[2048,1024]{1,0:T(8,128)} %param.5, f32[1024,128]{0,1:T(8,128)} %all-reduce.4.cloned.1.call-done), kind=kOutput, calls=%fused_computation | convolution fusion | flops 3221356544 | bytes 9961472 | tf_op jit(solution)/shard_map/dot_general | solution.py:66
  259.7 0.0 reduce-scatter.2.cloned.1.call-update
  259.7 0.0 all-reduce.6.cloned.1.call-start
  259.7 55.3 %reduce-scatter.2.cloned.1.call-done = f32[128,128]{0,1:T(8,128)} async-done(((f32[2048,128]{0,1:T(8,128)}), f32[128,128]{0,1:T(8,128)}) %reduce-scatter.2.cloned.1.call-update) | async-done | bytes 65552 | tf_op jit(solution)/shard_map/reduce_scatter | solution.py:65
  315.1 1.8 fusion.24
  316.9 0.0 all-reduce.6.cloned.1.call-update
  316.9 0.0 all-reduce.8.cloned.1.call-start
  316.9 243.7 %all-reduce.6.cloned.1.call-done = f32[128,128]{0,1:T(8,128)} async-done(((f32[128,128]{0,1:T(8,128)}), f32[128,128]{0,1:T(8,128)}) %all-reduce.6.cloned.1.call-update) | async-done | bytes 65552 | tf_op jit(solution)/shard_map/psum | solution.py:51
  560.6 0.9 copy.5
  561.6 0.9 fusion.7
  562.4 11.7 %cholesky.44 = f32[128,128]{1,0:T(8,128)S(1)} custom-call(f32[128,128]{1,0:T(8,128)S(1)} %fusion.7), custom_call_target="Cholesky" | custom-call | tf_op jit(solution)/shard_map/jit(cholesky)/cholesky | solution.py:36
  574.2 0.6 compare_reduce_fusion.1
  574.8 0.7 fusion.11
  575.5 9.8 %custom-call.6 = f32[1,128,128]{1,2,0:T(8,128)S(1)} custom-call(f32[1,128,128]{2,1,0:T(8,128)S(1)} %fusion.11), custom_call_target="InvertDiagBlocksLowerTriangular" | custom-call | tf_op jit(solution)/shard_map/triangular_solve/custom-call.0 | solution.py:37
  585.3 1.1 convolution_bitcast_fusion.3
  586.4 0.9 fusion.25
  587.3 0.0 all-reduce.8.cloned.1.call-update
  587.3 234.2 %all-reduce.8.cloned.1.call-done = f32[128,128]{0,1:T(8,128)} async-done(((f32[128,128]{0,1:T(8,128)}), f32[128,128]{0,1:T(8,128)}) %all-reduce.8.cloned.1.call-update) | async-done | bytes 65552 | tf_op jit(solution)/shard_map/psum | solution.py:51
  821.6 0.9 copy.7
  822.5 0.9 fusion.5
  823.4 11.7 %cholesky.55 = f32[128,128]{1,0:T(8,128)S(1)} custom-call(f32[128,128]{1,0:T(8,128)S(1)} %fusion.5), custom_call_target="Cholesky" | custom-call | tf_op jit(solution)/shard_map/jit(cholesky)/cholesky | solution.py:40
  835.1 0.7 compare_reduce_fusion
  835.9 2.3 convolution_multiply_fusion
  838.1 0.7 select_bitcast_fusion
  838.8 9.8 %custom-call.7 = f32[1,128,128]{1,2,0:T(8,128)S(1)} custom-call(f32[1,128,128]{2,1,0:T(8,128)S(1)} %select_bitcast_fusion), custom_call_target="InvertDiagBlocksLowerTriangular" | custom-call | tf_op jit(solution)/shard_map/triangular_solve/custom-call.0 | solution.py:41
  848.6 0.3 fusion
  848.9 0.7 copy.8
  (2 shorter events, 0.1 us)
Async XLA Ops:
  7.2 1.0 copy-start
  7.2 239.5 %all-reduce.4.cloned.1.call-start = ((), (), s32[]{:S(2)}) async-start(), calls=%async_computation.1 | async-start | bytes 1048576 | tf_op jit(solution)/shard_map/psum | solution.py:64
  8.2 139.1 %copy-start.1 = (f32[2048,1024]{1,0:T(8,128)S(1)}, f32[2048,1024]{1,0:T(8,128)}, u32[]{:S(2)}) copy-start(f32[2048,1024]{1,0:T(8,128)} %param.5) | copy-start | bytes 25165828
  18.1 5.6 collective-permute-start
  23.9 24.5 %collective-permute-start.1 = (f32[2048,128]{1,0:T(8,128)S(1)}, f32[2048,128]{1,0:T(8,128)S(1)}, u32[]{:S(2)}, u32[]{:S(2)}) collective-permute-start(f32[2048,128]{1,0:T(8,128)S(1)} %add.28), channel_id=1, source_target_pairs={{0,2},{1,3},{2,0},{3,1},{4,6},{5,7},{6,4},{7,5},{8,10},{9,11},{10,... | collective-permute-start | bytes 3145736 | tf_op jit(solution)/shard_map/ppermute | solution.py:16
  48.4 48.2 %collective-permute-start.2 = (f32[2048,128]{1,0:T(8,128)S(1)}, f32[2048,128]{1,0:T(8,128)S(1)}, u32[]{:S(2)}, u32[]{:S(2)}) collective-permute-start(f32[2048,128]{1,0:T(8,128)S(1)} %add.29), channel_id=1, source_target_pairs={{0,4},{1,5},{2,6},{3,7},{4,0},{5,1},{6,2},{7,3},{8,12},{9,13},{10,... | collective-permute-start | bytes 3145736 | tf_op jit(solution)/shard_map/ppermute | solution.py:16
  96.8 50.5 %collective-permute-start.3 = (f32[2048,128]{1,0:T(8,128)S(1)}, f32[2048,128]{1,0:T(8,128)S(1)}, u32[]{:S(2)}, u32[]{:S(2)}) collective-permute-start(f32[2048,128]{1,0:T(8,128)S(1)} %add.30), channel_id=1, source_target_pairs={{0,8},{1,9},{2,10},{3,11},{4,12},{5,13},{6,14},{7,15},{8,0},{9,1},... | collective-permute-start | bytes 3145736 | tf_op jit(solution)/shard_map/ppermute | solution.py:16
  152.8 162.3 %reduce-scatter.2.cloned.1.call-start = ((), (), s32[]{:S(2)}) async-start(), calls=%async_computation.2 | async-start | bytes 1114112 | tf_op jit(solution)/shard_map/reduce_scatter | solution.py:65
  259.7 301.0 %all-reduce.6.cloned.1.call-start = ((), (), s32[]{:S(2)}) async-start(), calls=%async_computation.3 | async-start | bytes 131072 | tf_op jit(solution)/shard_map/psum | solution.py:51
  316.9 504.7 %all-reduce.8.cloned.1.call-start = ((), (), s32[]{:S(2)}) async-start(), calls=%async_computation.4 | async-start | bytes 131072 | tf_op jit(solution)/shard_map/psum | solution.py:51
Sparse Core Ops, SparseCore 0:
  152.9 93.7 all-reduce.3
  259.8 55.2 reduce-scatter.1
  321.1 239.4 all-reduce.5
  587.5 234.0 all-reduce.7
